TPU v7x, 128 devices: a whole 4x4x4 slice. The times are simulated.
128 devices in a mesh: row: 16 (over y, x), col: 8 (over z, core).
Axes of the slice: x: 4, y: 4, z: 4, core: 2. Of those that a mesh axis runs over, the one named last changes fastest.
Arguments:
- statistic: float32 [16384, 16384], P('row', 'col'), may hold values from -6 to 6
- noise: bfloat16 [16384, 16384], P('row', 'col'), may hold values from -12 to 12
- grads: bfloat16 [16384, 4096], P('row', 'col'), may hold values from -1.5 to 1.5
Outputs:
- updated: float32 [16384, 16384], P('row', 'col')
All inputs are finite; a program needn't handle non-finite values.
Results may differ from a plain program's by a relative error of at most 0.0003.
Values may be sent and summed in bfloat16 or wider, within the bound.
No kernel may reach another device: no remote copies, remote signals or barrier semaphores. Data moves between devices by JAX's collectives and lax.ppermute only.
A program may use at most 640 MiB of HBM per device.

v0:
```python
import functools

import jax
import jax.numpy as jnp
from jax import lax
from jax.experimental import pallas as pl
from jax.experimental.pallas import tpu as pltpu
from jax.sharding import PartitionSpec as P

AXES = ("row", "col")
SIDE = 4
ORDER = (0, 1, 3, 2)
ROWS_TILE = 512
STREAMS = 2


def place(y, x, z, core):
    return (y % SIDE * SIDE + x % SIDE) * 2 * SIDE + z % SIDE * 2 + core


def coords():
    for y in range(SIDE):
        for x in range(SIDE):
            for z in range(SIDE):
                for core in range(2):
                    yield y, x, z, core


def turn(t):
    return t if t % 2 else (t + 2) % SIDE


def spread_pairs():
    pairs = []
    for y, x, z, core in coords():
        half = x // 2
        to_x = x if core == half else SIDE - 1 - x
        pairs.append((place(y, x, z, core), place(y + turn((z - y) % SIDE), to_x, y, half)))
    return pairs


def shift_pairs(step, first):
    pairs = []
    for y, x, z, core in coords():
        along_x = (core == 0) == first
        to = place(y, x - step, z, core) if along_x else place(y - step, x, z, core)
        pairs.append((place(y, x, z, core), to))
    return pairs


def unit_ids(offsets):
    row, col = lax.axis_index("row"), lax.axis_index("col")
    y, x, z, core = row // SIDE, row % SIDE, col // 2, col % 2
    blocks, eighths = [], []
    for j in offsets:
        for i in ORDER:
            uy = (y + jnp.where(core == 0, j, i)) % SIDE
            ux = (x + jnp.where(core == 0, i, j)) % SIDE
            t = (uy - z) % SIDE
            k = (z + jnp.where(t % 2 == 1, t, (t + 2) % SIDE)) % SIDE
            home = ux // 2 == core
            source_x = jnp.where(home, ux, SIDE - 1 - ux)
            blocks.append(source_x % 2)
            eighths.append(2 * k + jnp.where(home, core, 1 - core))
    return blocks, eighths, [row, col]


def tables(held):
    blocks, eighths, place_ids = held
    ones = sum(blocks)
    zeros = len(blocks) - ones
    slots, seen = [], jnp.int32(0)
    for n, block in enumerate(blocks):
        slots.append(jnp.where(block == 1, zeros + seen, n - seen))
        seen = seen + block
    return jnp.stack(slots + eighths + [zeros] + place_ids).astype(jnp.int32)


def blend_kernel(streams, pieces, fresh, table, panel, *refs):
    count = 1 + max(g for units in pieces for g, _ in units)
    groups, refs = refs[:count], refs[count:]
    carried, refs = refs[: 2 if fresh else 1], refs[2 if fresh else 1 :]
    out, left, right, tiles, added, lookup, left_sems, right_sems, in_sems, out_sems = refs[-10:]
    sources = [[groups[g].at[s] for g, s in units] for units in pieces]
    n = len(sources[0])
    eighths, rows, depth = left.shape
    width = right.shape[1]
    tile = tiles.shape[1]
    steps = [(m, q, b) for m in range(rows // tile) for q in range(len(streams)) for b in range(2)]

    def copy_right(q, u):
        slot = q * n + table[u]
        return pltpu.make_async_copy(sources[q][u], right.at[slot], right_sems.at[slot])

    def copy_left(s, m):
        eighth, span = s if fresh else table[n + s], pl.ds(m * tile, tile)
        return pltpu.make_async_copy(panel.at[eighth, span], left.at[s, span], left_sems.at[m, s])

    def window(ref, m, q, b):
        return ref.at[pl.ds(m * tile, tile), pl.ds((STREAMS * b + streams[q]) * width, width)]

    def copies_in(t):
        copies = [pltpu.make_async_copy(window(carried[0], *steps[t]), tiles.at[t], in_sems.at[0, t])]
        if fresh:
            copies.append(pltpu.make_async_copy(window(carried[1], *steps[t]), added.at[t], in_sems.at[1, t]))
        return copies

    def copy_out(t):
        return pltpu.make_async_copy(tiles.at[t], window(out, *steps[t]), out_sems.at[t])

    for s in range(eighths):
        copy_left(s, 0).start()
    lead = 1 if fresh else 3
    for t in range(lead):
        for copy in copies_in(t):
            copy.start()
    for q in range(len(streams)):
        for u in range(n):
            copy_right(q, u).start()
    for u in range(n):
        lookup[table[u]] = table[n + u] if fresh else u

    zeros = table[2 * n]
    for t, (m, q, b) in enumerate(steps):
        first = q == 0 and b == 0
        if first:
            for s in range(eighths):
                copy_left(s, m).wait()
        for copy in copies_in(t):
            copy.wait()
        if first and m + 1 < rows // tile:
            for s in range(eighths):
                copy_left(s, m + 1).start()
        if t + lead < len(steps):
            for copy in copies_in(t + lead):
                copy.start()
        if fresh:
            tiles[t] = 0.9 * tiles[t] + 0.1 * added[t].astype(jnp.float32)

        def pair(p, _):
            if m == 0:
                for s in range(2):
                    slot = q * n + 2 * p + s
                    pltpu.make_async_copy(sources[0][0], right.at[slot], right_sems.at[slot]).wait()
            parts = [
                lax.dot_general(
                    left[lookup[2 * p + s], m * tile : (m + 1) * tile, :],
                    right[q * n + 2 * p + s],
                    (((1,), (1,)), ((), ())),
                    preferred_element_type=jnp.float32,
                )
                for s in range(2)
            ]
            tiles[t] += 0.1 * (parts[0] + parts[1])
            return 0

        lax.fori_loop(0 if b == 0 else zeros // 2, zeros // 2 if b == 0 else n // 2, pair, 0)
        top = table[2 * n + 1] * rows + m * tile
        side = (table[2 * n + 2] * 2 + b) * (width * STREAMS) + streams[q] * width

        @pl.when(top < side + width - 1)
        def _():
            at_row = top + lax.broadcasted_iota(jnp.int32, (tile, width), 0)
            at_col = side + lax.broadcasted_iota(jnp.int32, (tile, width), 1)
            tiles[t] = jnp.where(at_row >= at_col, tiles[t], 0.0)

        copy_out(t).start()
    for t in range(len(steps)):
        copy_out(t).wait()


def blend(streams, pieces, table, panel, groups, fresh, before):
    eighths, rows, depth = panel.shape
    n, width = len(pieces[0]), groups[0].shape[1]
    held = n if fresh is None else eighths
    count = 2 * len(streams) * rows // ROWS_TILE
    carried = [before] if fresh is None else list(fresh)
    extra = [] if fresh is None or before is None else [before]
    operands = [table, panel, *groups, *carried, *extra]
    anywhere = pl.BlockSpec(memory_space=pl.ANY)
    return pl.pallas_call(
        functools.partial(blend_kernel, streams, pieces, fresh is not None),
        in_specs=[pl.BlockSpec(memory_space=pltpu.SMEM)] + [anywhere] * (len(operands) - 1),
        out_specs=anywhere,
        scratch_shapes=[
            pltpu.VMEM((held, rows, depth), jnp.bfloat16),
            pltpu.VMEM((len(streams) * n, width, depth), jnp.bfloat16),
            pltpu.VMEM((count, ROWS_TILE, width), jnp.float32),
            pltpu.VMEM((count if fresh else 1, ROWS_TILE, width), jnp.bfloat16),
            pltpu.SMEM((n,), jnp.int32),
            pltpu.SemaphoreType.DMA((rows // ROWS_TILE, held)),
            pltpu.SemaphoreType.DMA((len(streams) * n,)),
            pltpu.SemaphoreType.DMA((2, count)),
            pltpu.SemaphoreType.DMA((count,)),
        ],
        out_shape=jax.ShapeDtypeStruct((rows, 2 * STREAMS * width), jnp.float32),
        input_output_aliases={} if before is None else {len(operands) - 1: 0},
        compiler_params=pltpu.CompilerParams(vmem_limit_bytes=58 * 2**20),
        cost_estimate=pl.CostEstimate(
            flops=2 * len(streams) * n * rows * width * depth, bytes_accessed=24 * 2**20, transcendentals=0
        ),
    )(*operands)


def halves_kernel(ahead, behind, low, high, held, sems):
    count = low.shape[0]
    pairs = [(ahead.at[s], low.at[s]) for s in range(count)] + [(behind.at[count + s], high.at[s]) for s in range(count)]
    loads = [pltpu.make_async_copy(a, held.at[n], sems.at[0, n]) for n, (a, _) in enumerate(pairs)]
    stores = [pltpu.make_async_copy(held.at[n], b, sems.at[1, n]) for n, (_, b) in enumerate(pairs)]
    for load in loads:
        load.start()
    for load, store in zip(loads, stores):
        load.wait()
        store.start()
    for store in stores:
        store.wait()


def halves(ahead, behind):
    count, width, depth = ahead.shape
    half = jax.ShapeDtypeStruct((count // 2, width, depth), ahead.dtype)
    anywhere = pl.BlockSpec(memory_space=pl.ANY)
    return pl.pallas_call(
        halves_kernel,
        in_specs=[anywhere, anywhere],
        out_specs=[anywhere, anywhere],
        out_shape=[half, half],
        scratch_shapes=[pltpu.VMEM((count, width, depth), ahead.dtype), pltpu.SemaphoreType.DMA((2, count))],
        compiler_params=pltpu.CompilerParams(vmem_limit_bytes=58 * 2**20),
        cost_estimate=pl.CostEstimate(flops=0, bytes_accessed=4 * 2**20, transcendentals=0),
    )(ahead, behind)


def move(array, pairs):
    return lax.ppermute(array, AXES, pairs)


def shards(statistic, noise, grads):
    part = grads.shape[0] // STREAMS
    first = move(grads[:part], spread_pairs())
    first, rest = lax.optimization_barrier((first, grads))
    panel = lax.all_gather(rest, "col", axis=0)
    heads = [first, move(rest[part:], spread_pairs())]
    near, far = tables(unit_ids((0, 1, 3))), tables(unit_ids((2,)))
    inputs = (statistic, noise)

    def gather(unit):
        own = jnp.stack([unit] + [move(unit, shift_pairs(i, True)) for i in (1, -1, 2)])
        return own, move(own, shift_pairs(1, False)), move(own, shift_pairs(-1, False))

    def forward(ahead, behind):
        low, high = halves(ahead, behind)
        return move(low, shift_pairs(1, False)), move(high, shift_pairs(-1, False))

    held = [gather(unit) for unit in heads]
    units = [tuple((g, s) for g in range(3) for s in range(SIDE))]
    distant = forward(*held[0][1:])
    total = blend((0,), units, near, panel, held[0], inputs, None)
    (own, ahead, behind), total = lax.optimization_barrier((held[1], total))
    distant += forward(ahead, behind)
    total = blend((1,), units, near, panel, (own, ahead, behind), inputs, total)
    units = [tuple((2 * q + g, s) for g in range(2) for s in range(2)) for q in range(STREAMS)]
    return blend((0, 1), units, far, panel, distant, None, total)


def solution(mesh):
    in_specs = (P("row", "col"), P("row", "col"), P("row", "col"))
    out_specs = P("row", "col")
    return jax.shard_map(shards, mesh=mesh, in_specs=in_specs, out_specs=out_specs, check_vma=False)
```

profile of v0, /device:TPU:25, one launch (start us, length us, event | category | flops | bytes accessed | tf_op | source)
XLA Modules:
  0.0 159.4 jit_solution(8591861567732573424)
XLA Ops:
  6.5 0.0 copy-start.1
  6.5 0.0 all-gather.3.cloned.1.call-start
  6.5 1.2 slice.6
  7.7 6.2 %collective-permute-start = (bf16[512,512]{1,0:T(8,128)(2,1)S(1)}, bf16[512,512]{1,0:T(8,128)(2,1)S(1)}, u32[]{:S(2)}, u32[]{:S(2)}) collective-permute-start(bf16[512,512]{1,0:T(8,128)(2,1)S(1)} %slice.6), channel_id=1, source_target_pairs={{0,64},{1,88},{2,32},{3,56},{4,0},{5,24},{6,96},{7,120},{8,72},{9,... | collective-permute-start | bytes 1572872 | tf_op jit(solution)/shard_map/ppermute | solution.py:235
  13.9 8.0 %collective-permute-done = bf16[512,512]{1,0:T(8,128)(2,1)S(1)} collective-permute-done((bf16[512,512]{1,0:T(8,128)(2,1)S(1)}, bf16[512,512]{1,0:T(8,128)(2,1)S(1)}, u32[]{:S(2)}, u32[]{:S(2)}) %collective-permute-start) | collective-permute-done | bytes 524320 | tf_op jit(solution)/shard_map/ppermute | solution.py:235
  21.9 0.0 all-gather.3.cloned.1.call-update
  21.9 0.0 copy-done.1
  22.0 6.2 %collective-permute-start.8 = (bf16[512,512]{1,0:T(8,128)(2,1)S(1)}, bf16[512,512]{1,0:T(8,128)(2,1)S(1)}, u32[]{:S(2)}, u32[]{:S(2)}) collective-permute-start(bf16[512,512]{1,0:T(8,128)(2,1)S(1)} %slice.7), channel_id=1, source_target_pairs={{0,64},{1,88},{2,32},{3,56},{4,0},{5,24},{6,96},{7,120},{8,72},{9,... | collective-permute-start | bytes 1572872 | tf_op jit(solution)/shard_map/ppermute | solution.py:235
  28.2 0.0 collective-permute-start.3
  28.2 1.2 collective-permute-start.2
  29.4 0.2 collective-permute-start.1
  29.7 13.6 %collective-permute-done.8 = bf16[512,512]{1,0:T(8,128)(2,1)S(1)} collective-permute-done((bf16[512,512]{1,0:T(8,128)(2,1)S(1)}, bf16[512,512]{1,0:T(8,128)(2,1)S(1)}, u32[]{:S(2)}, u32[]{:S(2)}) %collective-permute-start.8) | collective-permute-done | bytes 524320 | tf_op jit(solution)/shard_map/ppermute | solution.py:235
  43.3 0.0 collective-permute-start.11
  43.3 0.1 collective-permute-start.10
  43.4 0.0 collective-permute-done.3
  43.4 1.3 collective-permute-start.9
  44.8 10.5 %collective-permute-done.2 = bf16[512,512]{1,0:T(8,128)(2,1)S(1)} collective-permute-done((bf16[512,512]{1,0:T(8,128)(2,1)S(1)}, bf16[512,512]{1,0:T(8,128)(2,1)S(1)}, u32[]{:S(2)}, u32[]{:S(2)}) %collective-permute-start.2) | collective-permute-done | bytes 524320 | tf_op jit(solution)/shard_map/ppermute | solution.py:235
  55.3 0.0 collective-permute-done.1
  55.3 1.6 pad_maximum_fusion.refs_0_
  56.9 0.0 collective-permute-start.5
  56.9 2.7 %collective-permute-start.4 = (bf16[4,512,512]{2,1,0:T(8,128)(2,1)}, bf16[4,512,512]{2,1,0:T(8,128)(2,1)}, u32[]{:S(2)}, u32[]{:S(2)}) collective-permute-start(bf16[4,512,512]{2,1,0:T(8,128)(2,1)} %pad_maximum_fusion.refs_0_), channel_id=1, source_target_pairs={{0,96},{1,25},{2,98},{3,27},{4,100},{5,29},{6,102},{7,31},{8,104},... | collective-permute-start | bytes 6291464 | tf_op jit(solution)/shard_map/ppermute | solution.py:235
  59.5 0.0 collective-permute-done.11
  59.5 1.5 collective-permute-done.10
  61.0 0.0 collective-permute-done.9
  61.0 0.3 pad_maximum_fusion.1.refs_0_
  61.3 0.0 copy-start
  61.3 0.1 collective-permute-start.13
  61.4 11.3 %collective-permute-start.12 = (bf16[4,512,512]{2,1,0:T(8,128)(2,1)S(1)}, bf16[4,512,512]{2,1,0:T(8,128)(2,1)}, u32[]{:S(2)}, u32[]{:S(2)}) collective-permute-start(bf16[4,512,512]{2,1,0:T(8,128)(2,1)S(1)} %pad_maximum_fusion.1.refs_0_), channel_id=1, source_target_pairs={{0,96},{1,25},{2,98},{3,27},{4,100},{5,29},{6,102},{7,31},{8,104},... | collective-permute-start | bytes 6291464 | tf_op jit(solution)/shard_map/ppermute | solution.py:235
  72.6 0.6 stack.193.table
  73.2 21.6 %collective-permute-done.5.behind.refs_2_ = bf16[4,512,512]{2,1,0:T(8,128)(2,1)} collective-permute-done((bf16[4,512,512]{2,1,0:T(8,128)(2,1)}, bf16[4,512,512]{2,1,0:T(8,128)(2,1)}, u32[]{:S(2)}, u32[]{:S(2)}) %collective-permute-start.5) | collective-permute-done | bytes 2097184 | tf_op jit(solution)/shard_map/ppermute | solution.py:235
  94.8 0.0 collective-permute-done.4.ahead.refs_1_
  94.8 2.5 %shard_map.37 = (bf16[2,512,512]{2,1,0:T(8,128)(2,1)}, bf16[2,512,512]{2,1,0:T(8,128)(2,1)}) custom-call(bf16[4,512,512]{2,1,0:T(8,128)(2,1)} %collective-permute-done.4.ahead.refs_1_, bf16[4,512,512]{2,1,0:T(8,128)(2,1)} %collective-permute-done.5.behind.refs_2_), custom_call_target="tpu_custom_call" | custom-call | bytes 4194304 | tf_op jit(solution)/shard_map/pallas_call | solution.py:223
  97.3 0.0 copy-done
  97.3 1.8 %collective-permute-start.6 = (bf16[2,512,512]{2,1,0:T(8,128)(2,1)}, bf16[2,512,512]{2,1,0:T(8,128)(2,1)S(1)}, u32[]{:S(2)}, u32[]{:S(2)}) collective-permute-start(bf16[2,512,512]{2,1,0:T(8,128)(2,1)} %get-tuple-element.17), channel_id=1, source_target_pairs={{0,96},{1,25},{2,98},{3,27},{4,100},{5,29},{6,102},{7,31},{8,104},... | collective-permute-start | bytes 3145736 | tf_op jit(solution)/shard_map/ppermute | solution.py:235
  99.0 0.0 collective-permute-start.7
  99.0 0.0 all-gather.3.cloned.1.call-done
  99.0 15.9 %shard_map.38.refs_5_ = f32[1024,2048]{1,0:T(8,128)} custom-call(s32[27]{0:T(128)} %stack.193.table, bf16[8,1024,512]{2,1,0:T(8,128)(2,1)} %bitcast.45, bf16[4,512,512]{2,1,0:T(8,128)(2,1)} %pad_maximum_fusion.refs_0_, bf16[4,512,512]{2,1,0:T(8,128)(2,1)} %collective-permute-done.4.ahead.refs_1_, bf16[4,512,512]{2,1,0:T(8,128)(2,1)} %collective-permute-done.5.behind.refs_2_, ...), custom_call_target="tpu_custom_call" | custom-call | flops 6442450944 | bytes 25165824 | tf_op jit(solution)/shard_map/pallas_call | solution.py:181
  115.0 2.2 %collective-permute-done.13.behind.refs_2_ = bf16[4,512,512]{2,1,0:T(8,128)(2,1)} collective-permute-done((bf16[4,512,512]{2,1,0:T(8,128)(2,1)S(1)}, bf16[4,512,512]{2,1,0:T(8,128)(2,1)}, u32[]{:S(2)}, u32[]{:S(2)}) %collective-permute-start.13) | collective-permute-done | bytes 2097184 | tf_op jit(solution)/shard_map/ppermute | solution.py:235
  117.2 0.0 collective-permute-done.12.ahead.refs_1_
  117.2 2.5 %shard_map.39 = (bf16[2,512,512]{2,1,0:T(8,128)(2,1)}, bf16[2,512,512]{2,1,0:T(8,128)(2,1)}) custom-call(bf16[4,512,512]{2,1,0:T(8,128)(2,1)} %collective-permute-done.12.ahead.refs_1_, bf16[4,512,512]{2,1,0:T(8,128)(2,1)} %collective-permute-done.13.behind.refs_2_), custom_call_target="tpu_custom_call" | custom-call | bytes 4194304 | tf_op jit(solution)/shard_map/pallas_call | solution.py:223
  119.6 1.8 %collective-permute-start.14 = (bf16[2,512,512]{2,1,0:T(8,128)(2,1)}, bf16[2,512,512]{2,1,0:T(8,128)(2,1)S(1)}, u32[]{:S(2)}, u32[]{:S(2)}) collective-permute-start(bf16[2,512,512]{2,1,0:T(8,128)(2,1)} %get-tuple-element.21), channel_id=1, source_target_pairs={{0,96},{1,25},{2,98},{3,27},{4,100},{5,29},{6,102},{7,31},{8,104},... | collective-permute-start | bytes 3145736 | tf_op jit(solution)/shard_map/ppermute | solution.py:235
  121.4 0.0 collective-permute-start.15
  121.4 0.6 stack.157.table
  122.0 15.9 %shard_map.40.refs_4_ = f32[1024,2048]{1,0:T(8,128)} custom-call(s32[27]{0:T(128)} %stack.193.table, bf16[8,1024,512]{2,1,0:T(8,128)(2,1)} %bitcast.46, bf16[4,512,512]{2,1,0:T(8,128)(2,1)} %copy-done, bf16[4,512,512]{2,1,0:T(8,128)(2,1)} %collective-permute-done.12.ahead.refs_1_, ...), custom_call_target="tpu_custom_call", output_to_operand_aliasing={{}: (7, {})} | custom-call | flops 6442450944 | bytes 25165824 | tf_op jit(solution)/shard_map/pallas_call | solution.py:181
  137.9 0.0 collective-permute-done.6.refs_0_
  137.9 0.0 copy-start.2
  137.9 0.0 collective-permute-done.7.refs_1_
  138.0 0.1 collective-permute-done.14.refs_2_
  138.0 0.0 copy-start.3
  138.0 1.3 collective-permute-done.15.refs_3_
  139.3 0.0 copy-done.2
  139.3 0.0 copy-done.3
  139.3 0.0 copy-start.4
  139.3 1.0 copy-done.4
  140.3 12.2 %shard_map.41 = f32[1024,2048]{1,0:T(8,128)} custom-call(s32[11]{0:T(128)} %stack.157.table, bf16[8,1024,512]{2,1,0:T(8,128)(2,1)} %bitcast.47, bf16[2,512,512]{2,1,0:T(8,128)(2,1)} %copy-done.2, bf16[2,512,512]{2,1,0:T(8,128)(2,1)} %collective-permute-done.7.refs_1_, bf16[2,512,512]{2,1,0:T(8,128)(2,1)} %copy-done.3, ...), custom_call_target="tpu_custom_call", output_to_operand_aliasing={{}: (6, {})} | custom-call | flops 4294967296 | bytes 25165824 | tf_op jit(solution)/shard_map/pallas_call | solution.py:181
  (1 shorter events, 0.0 us)
Async XLA Ops:
  6.5 15.4 %copy-start.1 = (bf16[1024,512]{1,0:T(8,128)(2,1)S(1)}, bf16[1024,512]{1,0:T(8,128)(2,1)}, u32[]{:S(2)}) copy-start(bf16[1024,512]{1,0:T(8,128)(2,1)} %param.5) | copy-start | bytes 3145732
  6.5 92.5 %all-gather.3.cloned.1.call-start = ((), (), s32[]{:S(2)}) async-start(), calls=%async_computation | async-start | bytes 9437184 | tf_op jit(solution)/shard_map/all_gather | solution.py:242
  7.7 14.2 %collective-permute-start = (bf16[512,512]{1,0:T(8,128)(2,1)S(1)}, bf16[512,512]{1,0:T(8,128)(2,1)S(1)}, u32[]{:S(2)}, u32[]{:S(2)}) collective-permute-start(bf16[512,512]{1,0:T(8,128)(2,1)S(1)} %slice.6), channel_id=1, source_target_pairs={{0,64},{1,88},{2,32},{3,56},{4,0},{5,24},{6,96},{7,120},{8,72},{9,... | collective-permute-start | bytes 1572872 | tf_op jit(solution)/shard_map/ppermute | solution.py:235
  22.0 21.3 %collective-permute-start.8 = (bf16[512,512]{1,0:T(8,128)(2,1)S(1)}, bf16[512,512]{1,0:T(8,128)(2,1)S(1)}, u32[]{:S(2)}, u32[]{:S(2)}) collective-permute-start(bf16[512,512]{1,0:T(8,128)(2,1)S(1)} %slice.7), channel_id=1, source_target_pairs={{0,64},{1,88},{2,32},{3,56},{4,0},{5,24},{6,96},{7,120},{8,72},{9,... | collective-permute-start | bytes 1572872 | tf_op jit(solution)/shard_map/ppermute | solution.py:235
  28.2 15.2 %collective-permute-start.3 = (bf16[512,512]{1,0:T(8,128)(2,1)S(1)}, bf16[512,512]{1,0:T(8,128)(2,1)S(1)}, u32[]{:S(2)}, u32[]{:S(2)}) collective-permute-start(bf16[512,512]{1,0:T(8,128)(2,1)S(1)} %collective-permute-done), channel_id=1, source_target_pairs={{0,16},{1,65},{2,18},{3,67},{4,20},{5,69},{6,22},{7,71},{8,24},{9,... | collective-permute-start | bytes 1572872 | tf_op jit(solution)/shard_map/ppermute | solution.py:235
  28.2 27.0 %collective-permute-start.2 = (bf16[512,512]{1,0:T(8,128)(2,1)S(1)}, bf16[512,512]{1,0:T(8,128)(2,1)S(1)}, u32[]{:S(2)}, u32[]{:S(2)}) collective-permute-start(bf16[512,512]{1,0:T(8,128)(2,1)S(1)} %collective-permute-done), channel_id=1, source_target_pairs={{0,8},{1,33},{2,10},{3,35},{4,12},{5,37},{6,14},{7,39},{8,16},{9,4... | collective-permute-start | bytes 1572872 | tf_op jit(solution)/shard_map/ppermute | solution.py:235
  29.4 25.8 %collective-permute-start.1 = (bf16[512,512]{1,0:T(8,128)(2,1)S(1)}, bf16[512,512]{1,0:T(8,128)(2,1)S(1)}, u32[]{:S(2)}, u32[]{:S(2)}) collective-permute-start(bf16[512,512]{1,0:T(8,128)(2,1)S(1)} %collective-permute-done), channel_id=1, source_target_pairs={{0,24},{1,97},{2,26},{3,99},{4,28},{5,101},{6,30},{7,103},{8,0},{9... | collective-permute-start | bytes 1572872 | tf_op jit(solution)/shard_map/ppermute | solution.py:235
  43.3 16.2 %collective-permute-start.11 = (bf16[512,512]{1,0:T(8,128)(2,1)S(1)}, bf16[512,512]{1,0:T(8,128)(2,1)S(1)}, u32[]{:S(2)}, u32[]{:S(2)}) collective-permute-start(bf16[512,512]{1,0:T(8,128)(2,1)S(1)} %collective-permute-done.8), channel_id=1, source_target_pairs={{0,16},{1,65},{2,18},{3,67},{4,20},{5,69},{6,22},{7,71},{8,24},{9,... | collective-permute-start | bytes 1572872 | tf_op jit(solution)/shard_map/ppermute | solution.py:235
  43.3 17.7 %collective-permute-start.10 = (bf16[512,512]{1,0:T(8,128)(2,1)S(1)}, bf16[512,512]{1,0:T(8,128)(2,1)S(1)}, u32[]{:S(2)}, u32[]{:S(2)}) collective-permute-start(bf16[512,512]{1,0:T(8,128)(2,1)S(1)} %collective-permute-done.8), channel_id=1, source_target_pairs={{0,8},{1,33},{2,10},{3,35},{4,12},{5,37},{6,14},{7,39},{8,16},{9,4... | collective-permute-start | bytes 1572872 | tf_op jit(solution)/shard_map/ppermute | solution.py:235
  43.4 17.6 %collective-permute-start.9 = (bf16[512,512]{1,0:T(8,128)(2,1)S(1)}, bf16[512,512]{1,0:T(8,128)(2,1)S(1)}, u32[]{:S(2)}, u32[]{:S(2)}) collective-permute-start(bf16[512,512]{1,0:T(8,128)(2,1)S(1)} %collective-permute-done.8), channel_id=1, source_target_pairs={{0,24},{1,97},{2,26},{3,99},{4,28},{5,101},{6,30},{7,103},{8,0},{9... | collective-permute-start | bytes 1572872 | tf_op jit(solution)/shard_map/ppermute | solution.py:235
  56.9 37.9 %collective-permute-start.5 = (bf16[4,512,512]{2,1,0:T(8,128)(2,1)}, bf16[4,512,512]{2,1,0:T(8,128)(2,1)}, u32[]{:S(2)}, u32[]{:S(2)}) collective-permute-start(bf16[4,512,512]{2,1,0:T(8,128)(2,1)} %pad_maximum_fusion.refs_0_), channel_id=1, source_target_pairs={{0,32},{1,9},{2,34},{3,11},{4,36},{5,13},{6,38},{7,15},{8,40},{9,1... | collective-permute-start | bytes 6291464 | tf_op jit(solution)/shard_map/ppermute | solution.py:235
  56.9 37.9 %collective-permute-start.4 = (bf16[4,512,512]{2,1,0:T(8,128)(2,1)}, bf16[4,512,512]{2,1,0:T(8,128)(2,1)}, u32[]{:S(2)}, u32[]{:S(2)}) collective-permute-start(bf16[4,512,512]{2,1,0:T(8,128)(2,1)} %pad_maximum_fusion.refs_0_), channel_id=1, source_target_pairs={{0,96},{1,25},{2,98},{3,27},{4,100},{5,29},{6,102},{7,31},{8,104},... | collective-permute-start | bytes 6291464 | tf_op jit(solution)/shard_map/ppermute | solution.py:235
  61.3 36.0 %copy-start = (bf16[4,512,512]{2,1,0:T(8,128)(2,1)}, bf16[4,512,512]{2,1,0:T(8,128)(2,1)S(1)}, u32[]{:S(2)}) copy-start(bf16[4,512,512]{2,1,0:T(8,128)(2,1)S(1)} %pad_maximum_fusion.1.refs_0_) | copy-start | bytes 6291460
  61.3 55.9 %collective-permute-start.13 = (bf16[4,512,512]{2,1,0:T(8,128)(2,1)S(1)}, bf16[4,512,512]{2,1,0:T(8,128)(2,1)}, u32[]{:S(2)}, u32[]{:S(2)}) collective-permute-start(bf16[4,512,512]{2,1,0:T(8,128)(2,1)S(1)} %pad_maximum_fusion.1.refs_0_), channel_id=1, source_target_pairs={{0,32},{1,9},{2,34},{3,11},{4,36},{5,13},{6,38},{7,15},{8,40},{9,1... | collective-permute-start | bytes 6291464 | tf_op jit(solution)/shard_map/ppermute | solution.py:235
  61.4 55.8 %collective-permute-start.12 = (bf16[4,512,512]{2,1,0:T(8,128)(2,1)S(1)}, bf16[4,512,512]{2,1,0:T(8,128)(2,1)}, u32[]{:S(2)}, u32[]{:S(2)}) collective-permute-start(bf16[4,512,512]{2,1,0:T(8,128)(2,1)S(1)} %pad_maximum_fusion.1.refs_0_), channel_id=1, source_target_pairs={{0,96},{1,25},{2,98},{3,27},{4,100},{5,29},{6,102},{7,31},{8,104},... | collective-permute-start | bytes 6291464 | tf_op jit(solution)/shard_map/ppermute | solution.py:235
  97.3 40.7 %collective-permute-start.6 = (bf16[2,512,512]{2,1,0:T(8,128)(2,1)}, bf16[2,512,512]{2,1,0:T(8,128)(2,1)S(1)}, u32[]{:S(2)}, u32[]{:S(2)}) collective-permute-start(bf16[2,512,512]{2,1,0:T(8,128)(2,1)} %get-tuple-element.17), channel_id=1, source_target_pairs={{0,96},{1,25},{2,98},{3,27},{4,100},{5,29},{6,102},{7,31},{8,104},... | collective-permute-start | bytes 3145736 | tf_op jit(solution)/shard_map/ppermute | solution.py:235
  99.0 38.9 %collective-permute-start.7 = (bf16[2,512,512]{2,1,0:T(8,128)(2,1)}, bf16[2,512,512]{2,1,0:T(8,128)(2,1)}, u32[]{:S(2)}, u32[]{:S(2)}) collective-permute-start(bf16[2,512,512]{2,1,0:T(8,128)(2,1)} %get-tuple-element.18), channel_id=1, source_target_pairs={{0,32},{1,9},{2,34},{3,11},{4,36},{5,13},{6,38},{7,15},{8,40},{9,1... | collective-permute-start | bytes 3145736 | tf_op jit(solution)/shard_map/ppermute | solution.py:235
  119.6 18.4 %collective-permute-start.14 = (bf16[2,512,512]{2,1,0:T(8,128)(2,1)}, bf16[2,512,512]{2,1,0:T(8,128)(2,1)S(1)}, u32[]{:S(2)}, u32[]{:S(2)}) collective-permute-start(bf16[2,512,512]{2,1,0:T(8,128)(2,1)} %get-tuple-element.21), channel_id=1, source_target_pairs={{0,96},{1,25},{2,98},{3,27},{4,100},{5,29},{6,102},{7,31},{8,104},... | collective-permute-start | bytes 3145736 | tf_op jit(solution)/shard_map/ppermute | solution.py:235
  121.4 17.9 %collective-permute-start.15 = (bf16[2,512,512]{2,1,0:T(8,128)(2,1)}, bf16[2,512,512]{2,1,0:T(8,128)(2,1)S(1)}, u32[]{:S(2)}, u32[]{:S(2)}) collective-permute-start(bf16[2,512,512]{2,1,0:T(8,128)(2,1)} %get-tuple-element.22), channel_id=1, source_target_pairs={{0,32},{1,9},{2,34},{3,11},{4,36},{5,13},{6,38},{7,15},{8,40},{9,1... | collective-permute-start | bytes 3145736 | tf_op jit(solution)/shard_map/ppermute | solution.py:235
  137.9 1.4 copy-start.2
  138.0 1.3 copy-start.3
  139.3 1.0 copy-start.4
Sparse Core Ops, SparseCore 0:
  22.1 65.3 all-gather.2
where the time goes:
time: 161 us; the launch traced here: 159 us
  waiting for transfers between devices  58.7 us (36%)
  Pallas kernels  48.9 us (30%)
  starting transfers between devices  33 us (20%)
  between operations  13.5 us (8%)
  local copies, waits for them, and re-layouts  3.43 us (2%)
  other arithmetic  1.84 us (1%)
    ppermute x16, waiting for transfers between devices, move(): return lax.ppermute(array, AXES, pairs)  58.7 us
    pallas_call x3, Pallas kernels, blend(): pl.pallas_call(functools.partial(blend_kernel, streams, pieces, fresh is...  44 us
    ppermute x16, starting transfers between devices, move(): return lax.ppermute(array, AXES, pairs)  33 us
    pallas_call x2, Pallas kernels, halves(): pl.pallas_call(halves_kernel, in_specs=[anywhere, anywhere], out_specs=[a...  4.91 us
  transfers between devices with their start and end apart: 17, of which 8 were waited for; matrix products, arithmetic and copies ran while one was open for 2% of the time, Pallas kernels for 23%

commit v1 on v0

--- a/solution.py
+++ b/solution.py
@@ -84,6 +84,7 @@
     sources = [[groups[g].at[s] for g, s in units] for units in pieces]
     n = len(sources[0])
     eighths, rows, depth = left.shape
+    every = n >= panel.shape[0]
     width = right.shape[1]
     tile = tiles.shape[1]
     steps = [(m, q, b) for m in range(rows // tile) for q in range(len(streams)) for b in range(2)]
@@ -93,7 +94,7 @@
         return pltpu.make_async_copy(sources[q][u], right.at[slot], right_sems.at[slot])
 
     def copy_left(s, m):
-        eighth, span = s if fresh else table[n + s], pl.ds(m * tile, tile)
+        eighth, span = s if every else table[n + s], pl.ds(m * tile, tile)
         return pltpu.make_async_copy(panel.at[eighth, span], left.at[s, span], left_sems.at[m, s])
 
     def window(ref, m, q, b):
@@ -110,7 +111,7 @@
 
     for s in range(eighths):
         copy_left(s, 0).start()
-    lead = 1 if fresh else 3
+    lead = 1 if len(streams) == 1 else 3
     for t in range(lead):
         for copy in copies_in(t):
             copy.start()
@@ -118,7 +119,7 @@
         for u in range(n):
             copy_right(q, u).start()
     for u in range(n):
-        lookup[table[u]] = table[n + u] if fresh else u
+        lookup[table[u]] = table[n + u] if every else u
 
     zeros = table[2 * n]
     for t, (m, q, b) in enumerate(steps):
@@ -172,7 +173,7 @@
 def blend(streams, pieces, table, panel, groups, fresh, before):
     eighths, rows, depth = panel.shape
     n, width = len(pieces[0]), groups[0].shape[1]
-    held = n if fresh is None else eighths
+    held = min(n, eighths)
     count = 2 * len(streams) * rows // ROWS_TILE
     carried = [before] if fresh is None else list(fresh)
     extra = [] if fresh is None or before is None else [before]
@@ -241,7 +242,7 @@
     first, rest = lax.optimization_barrier((first, grads))
     panel = lax.all_gather(rest, "col", axis=0)
     heads = [first, move(rest[part:], spread_pairs())]
-    near, far = tables(unit_ids((0, 1, 3))), tables(unit_ids((2,)))
+    mine, near, far = (tables(unit_ids(offsets)) for offsets in ((0,), (1, 3), (2,)))
     inputs = (statistic, noise)
 
     def gather(unit):
@@ -253,12 +254,14 @@
         return move(low, shift_pairs(1, False)), move(high, shift_pairs(-1, False))
 
     held = [gather(unit) for unit in heads]
-    units = [tuple((g, s) for g in range(3) for s in range(SIDE))]
-    distant = forward(*held[0][1:])
-    total = blend((0,), units, near, panel, held[0], inputs, None)
-    (own, ahead, behind), total = lax.optimization_barrier((held[1], total))
-    distant += forward(ahead, behind)
-    total = blend((1,), units, near, panel, (own, ahead, behind), inputs, total)
+    units = [tuple((q, s) for s in range(SIDE)) for q in range(STREAMS)]
+    total = blend((0, 1), units, mine, panel, [own for own, _, _ in held], inputs, None)
+    units = [tuple((g, s) for g in range(2) for s in range(SIDE))]
+    distant = ()
+    for stream, (_, ahead, behind) in enumerate(held):
+        (ahead, behind), total = lax.optimization_barrier(((ahead, behind), total))
+        distant += forward(ahead, behind)
+        total = blend((stream,), units, near, panel, (ahead, behind), None, total)
     units = [tuple((2 * q + g, s) for g in range(2) for s in range(2)) for q in range(STREAMS)]
     return blend((0, 1), units, far, panel, distant, None, total)
 

time: 161 us -> 169 us (1.050)
  Pallas kernels: 48.9 us -> 56.3 us
  waiting for transfers between devices: 58.7 us -> 56.7 us
    ppermute x16, waiting for transfers between devices: 58.7 us -> 45 us  [move(): return lax.ppermute(array, AXES, pairs)]
    all_gather x1, waiting for transfers between devices: 0.01 us -> 11.8 us  [shards(): panel = lax.all_gather(rest, 'col', axis=0)]
    pallas_call x3 -> x4, Pallas kernels: 44 us -> 51.5 us  [blend(): pl.pallas_call(functools.partial(blend_kernel, streams, pieces, fresh is...]
  transfers between devices with their start and end apart: 17 -> 17, of which waited for: 8 -> 7; matrix products, arithmetic and copies ran while one was open for 2% -> 2% of each run, Pallas kernels for 23% -> 25%
where the time goes in v1:
time: 169 us; the launch traced here: 166 us
  waiting for transfers between devices  56.7 us (34%)
  Pallas kernels  56.3 us (33%)
  starting transfers between devices  34.5 us (20%)
  between operations  13.6 us (8%)
  local copies, waits for them, and re-layouts  3.15 us (2%)
  other arithmetic  1.86 us (1%)
    pallas_call x4, Pallas kernels, blend(): pl.pallas_call(functools.partial(blend_kernel, streams, pieces, fresh is...  51.5 us
    ppermute x16, waiting for transfers between devices, move(): return lax.ppermute(array, AXES, pairs)  45 us
    ppermute x16, starting transfers between devices, move(): return lax.ppermute(array, AXES, pairs)  34.5 us
    all_gather x1, waiting for transfers between devices, shards(): panel = lax.all_gather(rest, 'col', axis=0)  11.8 us
    pallas_call x2, Pallas kernels, halves(): pl.pallas_call(halves_kernel, in_specs=[anywhere, anywhere], out_specs=[a...  4.85 us
  transfers between devices with their start and end apart: 17, of which 7 were waited for; matrix products, arithmetic and copies ran while one was open for 2% of the time, Pallas kernels for 25%

profile of v1, /device:TPU:25, one launch (start us, length us, event | category | flops | bytes accessed | tf_op | source)
XLA Modules:
  0.0 166.1 jit_solution(13506308875648379073)
XLA Ops:
  6.5 0.0 copy-start.1
  6.5 0.0 all-gather.3.cloned.1.call-start
  6.5 1.2 slice.6
  7.7 6.2 %collective-permute-start = (bf16[512,512]{1,0:T(8,128)(2,1)S(1)}, bf16[512,512]{1,0:T(8,128)(2,1)S(1)}, u32[]{:S(2)}, u32[]{:S(2)}) collective-permute-start(bf16[512,512]{1,0:T(8,128)(2,1)S(1)} %slice.6), channel_id=1, source_target_pairs={{0,64},{1,88},{2,32},{3,56},{4,0},{5,24},{6,96},{7,120},{8,72},{9,... | collective-permute-start | bytes 1572872 | tf_op jit(solution)/shard_map/ppermute | solution.py:236
  13.9 8.0 %collective-permute-done = bf16[512,512]{1,0:T(8,128)(2,1)S(1)} collective-permute-done((bf16[512,512]{1,0:T(8,128)(2,1)S(1)}, bf16[512,512]{1,0:T(8,128)(2,1)S(1)}, u32[]{:S(2)}, u32[]{:S(2)}) %collective-permute-start) | collective-permute-done | bytes 524320 | tf_op jit(solution)/shard_map/ppermute | solution.py:236
  21.9 0.0 all-gather.3.cloned.1.call-update
  21.9 0.0 copy-done.1
  22.0 6.2 %collective-permute-start.6 = (bf16[512,512]{1,0:T(8,128)(2,1)S(1)}, bf16[512,512]{1,0:T(8,128)(2,1)S(1)}, u32[]{:S(2)}, u32[]{:S(2)}) collective-permute-start(bf16[512,512]{1,0:T(8,128)(2,1)S(1)} %slice.7), channel_id=1, source_target_pairs={{0,64},{1,88},{2,32},{3,56},{4,0},{5,24},{6,96},{7,120},{8,72},{9,... | collective-permute-start | bytes 1572872 | tf_op jit(solution)/shard_map/ppermute | solution.py:236
  28.2 0.0 collective-permute-start.3
  28.2 1.2 collective-permute-start.2
  29.4 0.2 collective-permute-start.1
  29.7 13.6 %collective-permute-done.6 = bf16[512,512]{1,0:T(8,128)(2,1)S(1)} collective-permute-done((bf16[512,512]{1,0:T(8,128)(2,1)S(1)}, bf16[512,512]{1,0:T(8,128)(2,1)S(1)}, u32[]{:S(2)}, u32[]{:S(2)}) %collective-permute-start.6) | collective-permute-done | bytes 524320 | tf_op jit(solution)/shard_map/ppermute | solution.py:236
  43.3 0.0 collective-permute-start.9
  43.3 0.1 collective-permute-start.8
  43.4 0.0 collective-permute-done.3
  43.4 1.3 collective-permute-start.7
  44.8 10.5 %collective-permute-done.2 = bf16[512,512]{1,0:T(8,128)(2,1)S(1)} collective-permute-done((bf16[512,512]{1,0:T(8,128)(2,1)S(1)}, bf16[512,512]{1,0:T(8,128)(2,1)S(1)}, u32[]{:S(2)}, u32[]{:S(2)}) %collective-permute-start.2) | collective-permute-done | bytes 524320 | tf_op jit(solution)/shard_map/ppermute | solution.py:236
  55.3 0.0 collective-permute-done.1
  55.3 0.3 pad_maximum_fusion.refs_0_
  55.5 0.0 copy-start
  55.6 0.1 collective-permute-start.5
  55.6 2.7 %collective-permute-start.4 = (bf16[4,512,512]{2,1,0:T(8,128)(2,1)S(1)}, bf16[4,512,512]{2,1,0:T(8,128)(2,1)}, u32[]{:S(2)}, u32[]{:S(2)}) collective-permute-start(bf16[4,512,512]{2,1,0:T(8,128)(2,1)S(1)} %pad_maximum_fusion.refs_0_), channel_id=1, source_target_pairs={{0,96},{1,25},{2,98},{3,27},{4,100},{5,29},{6,102},{7,31},{8,104},... | collective-permute-start | bytes 6291464 | tf_op jit(solution)/shard_map/ppermute | solution.py:236
  58.4 0.0 collective-permute-done.9
  58.4 2.6 %collective-permute-done.8 = bf16[512,512]{1,0:T(8,128)(2,1)S(1)} collective-permute-done((bf16[512,512]{1,0:T(8,128)(2,1)S(1)}, bf16[512,512]{1,0:T(8,128)(2,1)S(1)}, u32[]{:S(2)}, u32[]{:S(2)}) %collective-permute-start.8) | collective-permute-done | bytes 524320 | tf_op jit(solution)/shard_map/ppermute | solution.py:236
  61.0 0.0 collective-permute-done.7
  61.0 1.6 pad_maximum_fusion.1.refs_1_
  62.6 0.0 copy-done
  62.6 0.0 collective-permute-start.13
  62.6 11.9 %collective-permute-start.12 = (bf16[4,512,512]{2,1,0:T(8,128)(2,1)}, bf16[4,512,512]{2,1,0:T(8,128)(2,1)}, u32[]{:S(2)}, u32[]{:S(2)}) collective-permute-start(bf16[4,512,512]{2,1,0:T(8,128)(2,1)} %pad_maximum_fusion.1.refs_1_), channel_id=1, source_target_pairs={{0,96},{1,25},{2,98},{3,27},{4,100},{5,29},{6,102},{7,31},{8,104},... | collective-permute-start | bytes 6291464 | tf_op jit(solution)/shard_map/ppermute | solution.py:236
  74.5 0.6 stack.180.table
  75.1 0.6 stack.203.table
  75.7 11.8 %all-gather.3.cloned.1.call-done = bf16[8192,512]{1,0:T(8,128)(2,1)} async-done(((bf16[1024,512]{1,0:T(8,128)(2,1)}), bf16[8192,512]{1,0:T(8,128)(2,1)}) %all-gather.3.cloned.1.call-update) | async-done | bytes 8388624 | tf_op jit(solution)/shard_map/all_gather | solution.py:243
  87.5 13.7 %shard_map.37.refs_2_ = f32[1024,2048]{1,0:T(8,128)} custom-call(s32[11]{0:T(128)} %stack.180.table, bf16[8,1024,512]{2,1,0:T(8,128)(2,1)} %bitcast.46, bf16[4,512,512]{2,1,0:T(8,128)(2,1)} %copy-done, bf16[4,512,512]{2,1,0:T(8,128)(2,1)} %pad_maximum_fusion.1.refs_1_, f32[1024,2048]{1,0:T(8,128)} %refs_2_.1, bf16[1024,2048]{1,0:T(8,128)(2,1)} %refs_3_.1), custom_call_target="tpu_custom_call" | custom-call | flops 4294967296 | bytes 25165824 | tf_op jit(solution)/shard_map/pallas_call | solution.py:182
  101.2 0.0 collective-permute-done.5.behind.refs_1_
  101.2 0.0 collective-permute-done.4.ahead.refs_0_
  101.3 2.4 %shard_map.38 = (bf16[2,512,512]{2,1,0:T(8,128)(2,1)}, bf16[2,512,512]{2,1,0:T(8,128)(2,1)}) custom-call(bf16[4,512,512]{2,1,0:T(8,128)(2,1)} %collective-permute-done.4.ahead.refs_0_, bf16[4,512,512]{2,1,0:T(8,128)(2,1)} %collective-permute-done.5.behind.refs_1_), custom_call_target="tpu_custom_call" | custom-call | bytes 4194304 | tf_op jit(solution)/shard_map/pallas_call | solution.py:224
  103.7 12.8 %shard_map.39.refs_2_ = f32[1024,2048]{1,0:T(8,128)} custom-call(s32[19]{0:T(128)} %stack.203.table, bf16[8,1024,512]{2,1,0:T(8,128)(2,1)} %bitcast.47, bf16[4,512,512]{2,1,0:T(8,128)(2,1)} %collective-permute-done.4.ahead.refs_0_, bf16[4,512,512]{2,1,0:T(8,128)(2,1)} %collective-permute-done.5.behind.refs_1_, ...), custom_call_target="tpu_custom_call", output_to_operand_aliasing={{}: (4, {})} | custom-call | flops 4294967296 | bytes 25165824 | tf_op jit(solution)/shard_map/pallas_call | solution.py:182
  116.5 0.0 collective-permute-done.13.behind.refs_1_
  116.5 0.0 collective-permute-done.12.ahead.refs_0_
  116.5 2.4 %shard_map.40 = (bf16[2,512,512]{2,1,0:T(8,128)(2,1)}, bf16[2,512,512]{2,1,0:T(8,128)(2,1)}) custom-call(bf16[4,512,512]{2,1,0:T(8,128)(2,1)} %collective-permute-done.12.ahead.refs_0_, bf16[4,512,512]{2,1,0:T(8,128)(2,1)} %collective-permute-done.13.behind.refs_1_), custom_call_target="tpu_custom_call" | custom-call | bytes 4194304 | tf_op jit(solution)/shard_map/pallas_call | solution.py:224
  118.9 1.7 %collective-permute-start.14 = (bf16[2,512,512]{2,1,0:T(8,128)(2,1)}, bf16[2,512,512]{2,1,0:T(8,128)(2,1)S(1)}, u32[]{:S(2)}, u32[]{:S(2)}) collective-permute-start(bf16[2,512,512]{2,1,0:T(8,128)(2,1)} %get-tuple-element.26), channel_id=1, source_target_pairs={{0,96},{1,25},{2,98},{3,27},{4,100},{5,29},{6,102},{7,31},{8,104},... | collective-permute-start | bytes 3145736 | tf_op jit(solution)/shard_map/ppermute | solution.py:236
  120.6 0.0 collective-permute-start.15
  120.6 2.7 %collective-permute-start.10 = (bf16[2,512,512]{2,1,0:T(8,128)(2,1)}, bf16[2,512,512]{2,1,0:T(8,128)(2,1)S(1)}, u32[]{:S(2)}, u32[]{:S(2)}) collective-permute-start(bf16[2,512,512]{2,1,0:T(8,128)(2,1)} %get-tuple-element.21), channel_id=1, source_target_pairs={{0,96},{1,25},{2,98},{3,27},{4,100},{5,29},{6,102},{7,31},{8,104},... | collective-permute-start | bytes 3145736 | tf_op jit(solution)/shard_map/ppermute | solution.py:236
  123.3 0.0 collective-permute-start.11
  123.3 0.7 stack.165.table
  124.0 12.8 %shard_map.41.refs_4_ = f32[1024,2048]{1,0:T(8,128)} custom-call(s32[19]{0:T(128)} %stack.203.table, bf16[8,1024,512]{2,1,0:T(8,128)(2,1)} %bitcast.48, bf16[4,512,512]{2,1,0:T(8,128)(2,1)} %collective-permute-done.12.ahead.refs_0_, bf16[4,512,512]{2,1,0:T(8,128)(2,1)} %collective-permute-done.13.behind.refs_1_, ...), custom_call_target="tpu_custom_call", output_to_operand_aliasing={{}: (4, {})} | custom-call | flops 4294967296 | bytes 25165824 | tf_op jit(solution)/shard_map/pallas_call | solution.py:182
  136.7 0.0 collective-permute-done.14.refs_2_
  136.7 0.0 copy-start.2
  136.8 0.0 collective-permute-done.15.refs_3_
  136.8 0.0 copy-start.3
  136.8 7.7 %collective-permute-done.10.refs_0_ = bf16[2,512,512]{2,1,0:T(8,128)(2,1)S(1)} collective-permute-done((bf16[2,512,512]{2,1,0:T(8,128)(2,1)}, bf16[2,512,512]{2,1,0:T(8,128)(2,1)S(1)}, u32[]{:S(2)}, u32[]{:S(2)}) %collective-permute-start.10) | collective-permute-done | bytes 1048608 | tf_op jit(solution)/shard_map/ppermute | solution.py:236
  144.5 0.0 copy-start.4
  144.5 2.5 %collective-permute-done.11.refs_1_ = bf16[2,512,512]{2,1,0:T(8,128)(2,1)} collective-permute-done((bf16[2,512,512]{2,1,0:T(8,128)(2,1)}, bf16[2,512,512]{2,1,0:T(8,128)(2,1)}, u32[]{:S(2)}, u32[]{:S(2)}) %collective-permute-start.11) | collective-permute-done | bytes 1048608 | tf_op jit(solution)/shard_map/ppermute | solution.py:236
  147.0 0.0 copy-done.2
  147.0 0.0 copy-done.3
  147.0 0.0 copy-done.4
  147.0 12.2 %shard_map.42 = f32[1024,2048]{1,0:T(8,128)} custom-call(s32[11]{0:T(128)} %stack.165.table, bf16[8,1024,512]{2,1,0:T(8,128)(2,1)} %bitcast.49, bf16[2,512,512]{2,1,0:T(8,128)(2,1)} %copy-done.4, bf16[2,512,512]{2,1,0:T(8,128)(2,1)} %collective-permute-done.11.refs_1_, bf16[2,512,512]{2,1,0:T(8,128)(2,1)} %copy-done.2, ...), custom_call_target="tpu_custom_call", output_to_operand_aliasing={{}: (6, {})} | custom-call | flops 4294967296 | bytes 25165824 | tf_op jit(solution)/shard_map/pallas_call | solution.py:182
  (1 shorter events, 0.0 us)
Async XLA Ops:
  6.5 15.4 %copy-start.1 = (bf16[1024,512]{1,0:T(8,128)(2,1)S(1)}, bf16[1024,512]{1,0:T(8,128)(2,1)}, u32[]{:S(2)}) copy-start(bf16[1024,512]{1,0:T(8,128)(2,1)} %param.5) | copy-start | bytes 3145732
  6.5 80.9 %all-gather.3.cloned.1.call-start = ((), (), s32[]{:S(2)}) async-start(), calls=%async_computation | async-start | bytes 9437184 | tf_op jit(solution)/shard_map/all_gather | solution.py:243
  7.7 14.2 %collective-permute-start = (bf16[512,512]{1,0:T(8,128)(2,1)S(1)}, bf16[512,512]{1,0:T(8,128)(2,1)S(1)}, u32[]{:S(2)}, u32[]{:S(2)}) collective-permute-start(bf16[512,512]{1,0:T(8,128)(2,1)S(1)} %slice.6), channel_id=1, source_target_pairs={{0,64},{1,88},{2,32},{3,56},{4,0},{5,24},{6,96},{7,120},{8,72},{9,... | collective-permute-start | bytes 1572872 | tf_op jit(solution)/shard_map/ppermute | solution.py:236
  22.0 21.3 %collective-permute-start.6 = (bf16[512,512]{1,0:T(8,128)(2,1)S(1)}, bf16[512,512]{1,0:T(8,128)(2,1)S(1)}, u32[]{:S(2)}, u32[]{:S(2)}) collective-permute-start(bf16[512,512]{1,0:T(8,128)(2,1)S(1)} %slice.7), channel_id=1, source_target_pairs={{0,64},{1,88},{2,32},{3,56},{4,0},{5,24},{6,96},{7,120},{8,72},{9,... | collective-permute-start | bytes 1572872 | tf_op jit(solution)/shard_map/ppermute | solution.py:236
  28.2 15.2 %collective-permute-start.3 = (bf16[512,512]{1,0:T(8,128)(2,1)S(1)}, bf16[512,512]{1,0:T(8,128)(2,1)S(1)}, u32[]{:S(2)}, u32[]{:S(2)}) collective-permute-start(bf16[512,512]{1,0:T(8,128)(2,1)S(1)} %collective-permute-done), channel_id=1, source_target_pairs={{0,16},{1,65},{2,18},{3,67},{4,20},{5,69},{6,22},{7,71},{8,24},{9,... | collective-permute-start | bytes 1572872 | tf_op jit(solution)/shard_map/ppermute | solution.py:236
  28.2 27.0 %collective-permute-start.2 = (bf16[512,512]{1,0:T(8,128)(2,1)S(1)}, bf16[512,512]{1,0:T(8,128)(2,1)S(1)}, u32[]{:S(2)}, u32[]{:S(2)}) collective-permute-start(bf16[512,512]{1,0:T(8,128)(2,1)S(1)} %collective-permute-done), channel_id=1, source_target_pairs={{0,8},{1,33},{2,10},{3,35},{4,12},{5,37},{6,14},{7,39},{8,16},{9,4... | collective-permute-start | bytes 1572872 | tf_op jit(solution)/shard_map/ppermute | solution.py:236
  29.4 25.8 %collective-permute-start.1 = (bf16[512,512]{1,0:T(8,128)(2,1)S(1)}, bf16[512,512]{1,0:T(8,128)(2,1)S(1)}, u32[]{:S(2)}, u32[]{:S(2)}) collective-permute-start(bf16[512,512]{1,0:T(8,128)(2,1)S(1)} %collective-permute-done), channel_id=1, source_target_pairs={{0,24},{1,97},{2,26},{3,99},{4,28},{5,101},{6,30},{7,103},{8,0},{9... | collective-permute-start | bytes 1572872 | tf_op jit(solution)/shard_map/ppermute | solution.py:236
  43.3 15.1 %collective-permute-start.9 = (bf16[512,512]{1,0:T(8,128)(2,1)S(1)}, bf16[512,512]{1,0:T(8,128)(2,1)S(1)}, u32[]{:S(2)}, u32[]{:S(2)}) collective-permute-start(bf16[512,512]{1,0:T(8,128)(2,1)S(1)} %collective-permute-done.6), channel_id=1, source_target_pairs={{0,16},{1,65},{2,18},{3,67},{4,20},{5,69},{6,22},{7,71},{8,24},{9,... | collective-permute-start | bytes 1572872 | tf_op jit(solution)/shard_map/ppermute | solution.py:236
  43.3 17.7 %collective-permute-start.8 = (bf16[512,512]{1,0:T(8,128)(2,1)S(1)}, bf16[512,512]{1,0:T(8,128)(2,1)S(1)}, u32[]{:S(2)}, u32[]{:S(2)}) collective-permute-start(bf16[512,512]{1,0:T(8,128)(2,1)S(1)} %collective-permute-done.6), channel_id=1, source_target_pairs={{0,8},{1,33},{2,10},{3,35},{4,12},{5,37},{6,14},{7,39},{8,16},{9,4... | collective-permute-start | bytes 1572872 | tf_op jit(solution)/shard_map/ppermute | solution.py:236
  43.4 17.6 %collective-permute-start.7 = (bf16[512,512]{1,0:T(8,128)(2,1)S(1)}, bf16[512,512]{1,0:T(8,128)(2,1)S(1)}, u32[]{:S(2)}, u32[]{:S(2)}) collective-permute-start(bf16[512,512]{1,0:T(8,128)(2,1)S(1)} %collective-permute-done.6), channel_id=1, source_target_pairs={{0,24},{1,97},{2,26},{3,99},{4,28},{5,101},{6,30},{7,103},{8,0},{9... | collective-permute-start | bytes 1572872 | tf_op jit(solution)/shard_map/ppermute | solution.py:236
  55.5 7.0 %copy-start = (bf16[4,512,512]{2,1,0:T(8,128)(2,1)}, bf16[4,512,512]{2,1,0:T(8,128)(2,1)S(1)}, u32[]{:S(2)}) copy-start(bf16[4,512,512]{2,1,0:T(8,128)(2,1)S(1)} %pad_maximum_fusion.refs_0_) | copy-start | bytes 6291460
  55.6 45.7 %collective-permute-start.5 = (bf16[4,512,512]{2,1,0:T(8,128)(2,1)S(1)}, bf16[4,512,512]{2,1,0:T(8,128)(2,1)}, u32[]{:S(2)}, u32[]{:S(2)}) collective-permute-start(bf16[4,512,512]{2,1,0:T(8,128)(2,1)S(1)} %pad_maximum_fusion.refs_0_), channel_id=1, source_target_pairs={{0,32},{1,9},{2,34},{3,11},{4,36},{5,13},{6,38},{7,15},{8,40},{9,1... | collective-permute-start | bytes 6291464 | tf_op jit(solution)/shard_map/ppermute | solution.py:236
  55.6 45.6 %collective-permute-start.4 = (bf16[4,512,512]{2,1,0:T(8,128)(2,1)S(1)}, bf16[4,512,512]{2,1,0:T(8,128)(2,1)}, u32[]{:S(2)}, u32[]{:S(2)}) collective-permute-start(bf16[4,512,512]{2,1,0:T(8,128)(2,1)S(1)} %pad_maximum_fusion.refs_0_), channel_id=1, source_target_pairs={{0,96},{1,25},{2,98},{3,27},{4,100},{5,29},{6,102},{7,31},{8,104},... | collective-permute-start | bytes 6291464 | tf_op jit(solution)/shard_map/ppermute | solution.py:236
  62.6 53.9 %collective-permute-start.13 = (bf16[4,512,512]{2,1,0:T(8,128)(2,1)}, bf16[4,512,512]{2,1,0:T(8,128)(2,1)}, u32[]{:S(2)}, u32[]{:S(2)}) collective-permute-start(bf16[4,512,512]{2,1,0:T(8,128)(2,1)} %pad_maximum_fusion.1.refs_1_), channel_id=1, source_target_pairs={{0,32},{1,9},{2,34},{3,11},{4,36},{5,13},{6,38},{7,15},{8,40},{9,1... | collective-permute-start | bytes 6291464 | tf_op jit(solution)/shard_map/ppermute | solution.py:236
  62.6 53.9 %collective-permute-start.12 = (bf16[4,512,512]{2,1,0:T(8,128)(2,1)}, bf16[4,512,512]{2,1,0:T(8,128)(2,1)}, u32[]{:S(2)}, u32[]{:S(2)}) collective-permute-start(bf16[4,512,512]{2,1,0:T(8,128)(2,1)} %pad_maximum_fusion.1.refs_1_), channel_id=1, source_target_pairs={{0,96},{1,25},{2,98},{3,27},{4,100},{5,29},{6,102},{7,31},{8,104},... | collective-permute-start | bytes 6291464 | tf_op jit(solution)/shard_map/ppermute | solution.py:236
  118.9 17.8 %collective-permute-start.14 = (bf16[2,512,512]{2,1,0:T(8,128)(2,1)}, bf16[2,512,512]{2,1,0:T(8,128)(2,1)S(1)}, u32[]{:S(2)}, u32[]{:S(2)}) collective-permute-start(bf16[2,512,512]{2,1,0:T(8,128)(2,1)} %get-tuple-element.26), channel_id=1, source_target_pairs={{0,96},{1,25},{2,98},{3,27},{4,100},{5,29},{6,102},{7,31},{8,104},... | collective-permute-start | bytes 3145736 | tf_op jit(solution)/shard_map/ppermute | solution.py:236
  120.6 16.2 %collective-permute-start.15 = (bf16[2,512,512]{2,1,0:T(8,128)(2,1)}, bf16[2,512,512]{2,1,0:T(8,128)(2,1)S(1)}, u32[]{:S(2)}, u32[]{:S(2)}) collective-permute-start(bf16[2,512,512]{2,1,0:T(8,128)(2,1)} %get-tuple-element.27), channel_id=1, source_target_pairs={{0,32},{1,9},{2,34},{3,11},{4,36},{5,13},{6,38},{7,15},{8,40},{9,1... | collective-permute-start | bytes 3145736 | tf_op jit(solution)/shard_map/ppermute | solution.py:236
  120.6 23.9 %collective-permute-start.10 = (bf16[2,512,512]{2,1,0:T(8,128)(2,1)}, bf16[2,512,512]{2,1,0:T(8,128)(2,1)S(1)}, u32[]{:S(2)}, u32[]{:S(2)}) collective-permute-start(bf16[2,512,512]{2,1,0:T(8,128)(2,1)} %get-tuple-element.21), channel_id=1, source_target_pairs={{0,96},{1,25},{2,98},{3,27},{4,100},{5,29},{6,102},{7,31},{8,104},... | collective-permute-start | bytes 3145736 | tf_op jit(solution)/shard_map/ppermute | solution.py:236
  123.3 23.7 %collective-permute-start.11 = (bf16[2,512,512]{2,1,0:T(8,128)(2,1)}, bf16[2,512,512]{2,1,0:T(8,128)(2,1)}, u32[]{:S(2)}, u32[]{:S(2)}) collective-permute-start(bf16[2,512,512]{2,1,0:T(8,128)(2,1)} %get-tuple-element.22), channel_id=1, source_target_pairs={{0,32},{1,9},{2,34},{3,11},{4,36},{5,13},{6,38},{7,15},{8,40},{9,1... | collective-permute-start | bytes 3145736 | tf_op jit(solution)/shard_map/ppermute | solution.py:236
  136.7 10.3 %copy-start.2 = (bf16[2,512,512]{2,1,0:T(8,128)(2,1)}, bf16[2,512,512]{2,1,0:T(8,128)(2,1)S(1)}, u32[]{:S(2)}) copy-start(bf16[2,512,512]{2,1,0:T(8,128)(2,1)S(1)} %collective-permute-done.14.refs_2_) | copy-start | bytes 3145732
  136.8 10.2 %copy-start.3 = (bf16[2,512,512]{2,1,0:T(8,128)(2,1)}, bf16[2,512,512]{2,1,0:T(8,128)(2,1)S(1)}, u32[]{:S(2)}) copy-start(bf16[2,512,512]{2,1,0:T(8,128)(2,1)S(1)} %collective-permute-done.15.refs_3_) | copy-start | bytes 3145732
  144.5 2.5 %copy-start.4 = (bf16[2,512,512]{2,1,0:T(8,128)(2,1)}, bf16[2,512,512]{2,1,0:T(8,128)(2,1)S(1)}, u32[]{:S(2)}) copy-start(bf16[2,512,512]{2,1,0:T(8,128)(2,1)S(1)} %collective-permute-done.10.refs_0_) | copy-start | bytes 3145732
Sparse Core Ops, SparseCore 0:
  22.1 65.3 all-gather.2

commit v2 on v0

--- a/solution.py
+++ b/solution.py
@@ -195,7 +195,7 @@
         ],
         out_shape=jax.ShapeDtypeStruct((rows, 2 * STREAMS * width), jnp.float32),
         input_output_aliases={} if before is None else {len(operands) - 1: 0},
-        compiler_params=pltpu.CompilerParams(vmem_limit_bytes=58 * 2**20),
+        compiler_params=pltpu.CompilerParams(vmem_limit_bytes=(58 if len(streams) == 1 else 48) * 2**20),
         cost_estimate=pl.CostEstimate(
             flops=2 * len(streams) * n * rows * width * depth, bytes_accessed=24 * 2**20, transcendentals=0
         ),

time: 161 us -> 156 us (0.969)
  waiting for transfers between devices: 58.7 us -> 55.3 us
  starting transfers between devices: 33 us -> 35.4 us
    ppermute x16, waiting for transfers between devices: 58.7 us -> 55.3 us  [move(): return lax.ppermute(array, AXES, pairs)]
    ppermute x16, starting transfers between devices: 33 us -> 35.4 us  [move(): return lax.ppermute(array, AXES, pairs)]
  transfers between devices with their start and end apart: 17 -> 17, of which waited for: 8 -> 8; matrix products, arithmetic and copies ran while one was open for 2% -> 2% of each run, Pallas kernels for 23% -> 24%
where the time goes in v2:
time: 156 us
  waiting for transfers between devices  55.3 us (35%)
  Pallas kernels  47.7 us (31%)
  starting transfers between devices  35.4 us (23%)
  between operations  13.5 us (9%)
  local copies, waits for them, and re-layouts  1.99 us (1%)
  other arithmetic  1.92 us (1%)
    ppermute x16, waiting for transfers between devices, move(): return lax.ppermute(array, AXES, pairs)  55.3 us
    pallas_call x3, Pallas kernels, blend(): pl.pallas_call(functools.partial(blend_kernel, streams, pieces, fresh is...  42.8 us
    ppermute x16, starting transfers between devices, move(): return lax.ppermute(array, AXES, pairs)  35.4 us
    pallas_call x2, Pallas kernels, halves(): pl.pallas_call(halves_kernel, in_specs=[anywhere, anywhere], out_specs=[a...  4.89 us
  transfers between devices with their start and end apart: 17, of which 8 were waited for; matrix products, arithmetic and copies ran while one was open for 2% of the time, Pallas kernels for 24%

profile of v2, /device:TPU:25, one launch (start us, length us, event | category | flops | bytes accessed | tf_op | source)
XLA Modules:
  0.0 155.9 jit_solution(10479316756284081801)
XLA Ops:
  6.5 0.0 copy-start.1
  6.5 0.0 all-gather.3.cloned.1.call-start
  6.5 1.2 slice.6
  7.7 6.2 %collective-permute-start = (bf16[512,512]{1,0:T(8,128)(2,1)S(1)}, bf16[512,512]{1,0:T(8,128)(2,1)S(1)}, u32[]{:S(2)}, u32[]{:S(2)}) collective-permute-start(bf16[512,512]{1,0:T(8,128)(2,1)S(1)} %slice.6), channel_id=1, source_target_pairs={{0,64},{1,88},{2,32},{3,56},{4,0},{5,24},{6,96},{7,120},{8,72},{9,... | collective-permute-start | bytes 1572872 | tf_op jit(solution)/shard_map/ppermute | solution.py:235
  13.9 8.0 %collective-permute-done = bf16[512,512]{1,0:T(8,128)(2,1)S(1)} collective-permute-done((bf16[512,512]{1,0:T(8,128)(2,1)S(1)}, bf16[512,512]{1,0:T(8,128)(2,1)S(1)}, u32[]{:S(2)}, u32[]{:S(2)}) %collective-permute-start) | collective-permute-done | bytes 524320 | tf_op jit(solution)/shard_map/ppermute | solution.py:235
  21.9 0.0 all-gather.3.cloned.1.call-update
  21.9 0.0 copy-done.1
  22.0 6.2 %collective-permute-start.8 = (bf16[512,512]{1,0:T(8,128)(2,1)S(1)}, bf16[512,512]{1,0:T(8,128)(2,1)S(1)}, u32[]{:S(2)}, u32[]{:S(2)}) collective-permute-start(bf16[512,512]{1,0:T(8,128)(2,1)S(1)} %slice.7), channel_id=1, source_target_pairs={{0,64},{1,88},{2,32},{3,56},{4,0},{5,24},{6,96},{7,120},{8,72},{9,... | collective-permute-start | bytes 1572872 | tf_op jit(solution)/shard_map/ppermute | solution.py:235
  28.2 0.0 collective-permute-start.3
  28.2 1.2 collective-permute-start.2
  29.4 0.2 collective-permute-start.1
  29.7 13.6 %collective-permute-done.8 = bf16[512,512]{1,0:T(8,128)(2,1)S(1)} collective-permute-done((bf16[512,512]{1,0:T(8,128)(2,1)S(1)}, bf16[512,512]{1,0:T(8,128)(2,1)S(1)}, u32[]{:S(2)}, u32[]{:S(2)}) %collective-permute-start.8) | collective-permute-done | bytes 524320 | tf_op jit(solution)/shard_map/ppermute | solution.py:235
  43.3 0.0 collective-permute-start.11
  43.3 0.1 collective-permute-start.10
  43.4 0.0 collective-permute-done.3
  43.4 1.3 collective-permute-start.9
  44.8 10.5 %collective-permute-done.2 = bf16[512,512]{1,0:T(8,128)(2,1)S(1)} collective-permute-done((bf16[512,512]{1,0:T(8,128)(2,1)S(1)}, bf16[512,512]{1,0:T(8,128)(2,1)S(1)}, u32[]{:S(2)}, u32[]{:S(2)}) %collective-permute-start.2) | collective-permute-done | bytes 524320 | tf_op jit(solution)/shard_map/ppermute | solution.py:235
  55.3 0.0 collective-permute-done.1
  55.3 0.3 pad_maximum_fusion.refs_0_
  55.5 0.0 copy-start
  55.6 0.1 collective-permute-start.5
  55.6 2.7 %collective-permute-start.4 = (bf16[4,512,512]{2,1,0:T(8,128)(2,1)S(1)}, bf16[4,512,512]{2,1,0:T(8,128)(2,1)}, u32[]{:S(2)}, u32[]{:S(2)}) collective-permute-start(bf16[4,512,512]{2,1,0:T(8,128)(2,1)S(1)} %pad_maximum_fusion.refs_0_), channel_id=1, source_target_pairs={{0,96},{1,25},{2,98},{3,27},{4,100},{5,29},{6,102},{7,31},{8,104},... | collective-permute-start | bytes 6291464 | tf_op jit(solution)/shard_map/ppermute | solution.py:235
  58.4 0.0 collective-permute-done.11
  58.4 2.6 %collective-permute-done.10 = bf16[512,512]{1,0:T(8,128)(2,1)S(1)} collective-permute-done((bf16[512,512]{1,0:T(8,128)(2,1)S(1)}, bf16[512,512]{1,0:T(8,128)(2,1)S(1)}, u32[]{:S(2)}, u32[]{:S(2)}) %collective-permute-start.10) | collective-permute-done | bytes 524320 | tf_op jit(solution)/shard_map/ppermute | solution.py:235
  61.0 0.0 collective-permute-done.9
  61.0 1.7 %pad_maximum_fusion.1.refs_0_ = bf16[4,512,512]{2,1,0:T(8,128)(2,1)} fusion(bf16[1,512,512]{2,1,0:T(8,128)(2,1)S(1)} %bitcast.50, bf16[1,512,512]{2,1,0:T(8,128)(2,1)S(1)} %bitcast.51, bf16[1,512,512]{2,1,0:T(8,128)(2,1)S(1)} %bitcast.54, bf16[1,512,512]{2,1,0:T(8,128)(2,1)S(1)} %bitcast.48), kind=kLoop, calls=%fused_computation.1 | loop fusion | flops 3145728 | bytes 4194304 | tf_op jit(solution)/shard_map/stack | solution.py:248
  62.6 0.0 copy-done
  62.6 0.0 collective-permute-start.13
  62.7 11.9 %collective-permute-start.12 = (bf16[4,512,512]{2,1,0:T(8,128)(2,1)}, bf16[4,512,512]{2,1,0:T(8,128)(2,1)}, u32[]{:S(2)}, u32[]{:S(2)}) collective-permute-start(bf16[4,512,512]{2,1,0:T(8,128)(2,1)} %pad_maximum_fusion.1.refs_0_), channel_id=1, source_target_pairs={{0,96},{1,25},{2,98},{3,27},{4,100},{5,29},{6,102},{7,31},{8,104},... | collective-permute-start | bytes 6291464 | tf_op jit(solution)/shard_map/ppermute | solution.py:235
  74.5 0.7 stack.193.table
  75.2 18.1 %collective-permute-done.5.behind.refs_2_ = bf16[4,512,512]{2,1,0:T(8,128)(2,1)} collective-permute-done((bf16[4,512,512]{2,1,0:T(8,128)(2,1)S(1)}, bf16[4,512,512]{2,1,0:T(8,128)(2,1)}, u32[]{:S(2)}, u32[]{:S(2)}) %collective-permute-start.5) | collective-permute-done | bytes 2097184 | tf_op jit(solution)/shard_map/ppermute | solution.py:235
  93.4 0.0 collective-permute-done.4.ahead.refs_1_
  93.4 2.5 %shard_map.37 = (bf16[2,512,512]{2,1,0:T(8,128)(2,1)}, bf16[2,512,512]{2,1,0:T(8,128)(2,1)}) custom-call(bf16[4,512,512]{2,1,0:T(8,128)(2,1)} %collective-permute-done.4.ahead.refs_1_, bf16[4,512,512]{2,1,0:T(8,128)(2,1)} %collective-permute-done.5.behind.refs_2_), custom_call_target="tpu_custom_call" | custom-call | bytes 4194304 | tf_op jit(solution)/shard_map/pallas_call | solution.py:223
  95.8 2.6 %collective-permute-start.6 = (bf16[2,512,512]{2,1,0:T(8,128)(2,1)}, bf16[2,512,512]{2,1,0:T(8,128)(2,1)S(1)}, u32[]{:S(2)}, u32[]{:S(2)}) collective-permute-start(bf16[2,512,512]{2,1,0:T(8,128)(2,1)} %get-tuple-element.17), channel_id=1, source_target_pairs={{0,96},{1,25},{2,98},{3,27},{4,100},{5,29},{6,102},{7,31},{8,104},... | collective-permute-start | bytes 3145736 | tf_op jit(solution)/shard_map/ppermute | solution.py:235
  98.5 0.0 collective-permute-start.7
  98.5 0.0 all-gather.3.cloned.1.call-done
  98.5 15.9 %shard_map.38.refs_5_ = f32[1024,2048]{1,0:T(8,128)} custom-call(s32[27]{0:T(128)} %stack.193.table, bf16[8,1024,512]{2,1,0:T(8,128)(2,1)} %bitcast.45, bf16[4,512,512]{2,1,0:T(8,128)(2,1)} %copy-done, bf16[4,512,512]{2,1,0:T(8,128)(2,1)} %collective-permute-done.4.ahead.refs_1_, bf16[4,512,512]{2,1,0:T(8,128)(2,1)} %collective-permute-done.5.behind.refs_2_, ...), custom_call_target="tpu_custom_call" | custom-call | flops 6442450944 | bytes 25165824 | tf_op jit(solution)/shard_map/pallas_call | solution.py:181
  114.4 1.3 collective-permute-done.13.behind.refs_2_
  115.7 0.0 collective-permute-done.12.ahead.refs_1_
  115.7 2.4 %shard_map.39 = (bf16[2,512,512]{2,1,0:T(8,128)(2,1)}, bf16[2,512,512]{2,1,0:T(8,128)(2,1)}) custom-call(bf16[4,512,512]{2,1,0:T(8,128)(2,1)} %collective-permute-done.12.ahead.refs_1_, bf16[4,512,512]{2,1,0:T(8,128)(2,1)} %collective-permute-done.13.behind.refs_2_), custom_call_target="tpu_custom_call" | custom-call | bytes 4194304 | tf_op jit(solution)/shard_map/pallas_call | solution.py:223
  118.2 2.6 %collective-permute-start.14 = (bf16[2,512,512]{2,1,0:T(8,128)(2,1)}, bf16[2,512,512]{2,1,0:T(8,128)(2,1)S(1)}, u32[]{:S(2)}, u32[]{:S(2)}) collective-permute-start(bf16[2,512,512]{2,1,0:T(8,128)(2,1)} %get-tuple-element.21), channel_id=1, source_target_pairs={{0,96},{1,25},{2,98},{3,27},{4,100},{5,29},{6,102},{7,31},{8,104},... | collective-permute-start | bytes 3145736 | tf_op jit(solution)/shard_map/ppermute | solution.py:235
  120.8 0.0 collective-permute-start.15
  120.8 0.1 stack.157.table
  120.9 15.9 %shard_map.40.refs_4_ = f32[1024,2048]{1,0:T(8,128)} custom-call(s32[27]{0:T(128)} %stack.193.table, bf16[8,1024,512]{2,1,0:T(8,128)(2,1)} %bitcast.46, bf16[4,512,512]{2,1,0:T(8,128)(2,1)} %pad_maximum_fusion.1.refs_0_, bf16[4,512,512]{2,1,0:T(8,128)(2,1)} %collective-permute-done.12.ahead.refs_1_, ...), custom_call_target="tpu_custom_call", output_to_operand_aliasing={{}: (7, {})} | custom-call | flops 6442450944 | bytes 25165824 | tf_op jit(solution)/shard_map/pallas_call | solution.py:181
  136.8 0.0 collective-permute-done.6.refs_0_
  136.8 0.0 collective-permute-done.7.refs_1_
  136.8 0.6 collective-permute-done.14.refs_2_
  137.5 0.5 collective-permute-done.15.refs_3_
  138.0 11.0 %shard_map.41 = f32[1024,2048]{1,0:T(8,128)} custom-call(s32[11]{0:T(128)S(1)} %stack.157.table, bf16[8,1024,512]{2,1,0:T(8,128)(2,1)} %bitcast.47, bf16[2,512,512]{2,1,0:T(8,128)(2,1)S(1)} %collective-permute-done.6.refs_0_, bf16[2,512,512]{2,1,0:T(8,128)(2,1)S(1)} %collective-permute-done.7.refs_1_, ...), custom_call_target="tpu_custom_call", output_to_operand_aliasing={{}: (6, {})} | custom-call | flops 4294967296 | bytes 25165824 | tf_op jit(solution)/shard_map/pallas_call | solution.py:181
  (1 shorter events, 0.0 us)
Async XLA Ops:
  6.5 15.4 %copy-start.1 = (bf16[1024,512]{1,0:T(8,128)(2,1)S(1)}, bf16[1024,512]{1,0:T(8,128)(2,1)}, u32[]{:S(2)}) copy-start(bf16[1024,512]{1,0:T(8,128)(2,1)} %param.5) | copy-start | bytes 3145732
  6.5 91.9 %all-gather.3.cloned.1.call-start = ((), (), s32[]{:S(2)}) async-start(), calls=%async_computation | async-start | bytes 9437184 | tf_op jit(solution)/shard_map/all_gather | solution.py:242
  7.7 14.2 %collective-permute-start = (bf16[512,512]{1,0:T(8,128)(2,1)S(1)}, bf16[512,512]{1,0:T(8,128)(2,1)S(1)}, u32[]{:S(2)}, u32[]{:S(2)}) collective-permute-start(bf16[512,512]{1,0:T(8,128)(2,1)S(1)} %slice.6), channel_id=1, source_target_pairs={{0,64},{1,88},{2,32},{3,56},{4,0},{5,24},{6,96},{7,120},{8,72},{9,... | collective-permute-start | bytes 1572872 | tf_op jit(solution)/shard_map/ppermute | solution.py:235
  22.0 21.3 %collective-permute-start.8 = (bf16[512,512]{1,0:T(8,128)(2,1)S(1)}, bf16[512,512]{1,0:T(8,128)(2,1)S(1)}, u32[]{:S(2)}, u32[]{:S(2)}) collective-permute-start(bf16[512,512]{1,0:T(8,128)(2,1)S(1)} %slice.7), channel_id=1, source_target_pairs={{0,64},{1,88},{2,32},{3,56},{4,0},{5,24},{6,96},{7,120},{8,72},{9,... | collective-permute-start | bytes 1572872 | tf_op jit(solution)/shard_map/ppermute | solution.py:235
  28.2 15.2 %collective-permute-start.3 = (bf16[512,512]{1,0:T(8,128)(2,1)S(1)}, bf16[512,512]{1,0:T(8,128)(2,1)S(1)}, u32[]{:S(2)}, u32[]{:S(2)}) collective-permute-start(bf16[512,512]{1,0:T(8,128)(2,1)S(1)} %collective-permute-done), channel_id=1, source_target_pairs={{0,16},{1,65},{2,18},{3,67},{4,20},{5,69},{6,22},{7,71},{8,24},{9,... | collective-permute-start | bytes 1572872 | tf_op jit(solution)/shard_map/ppermute | solution.py:235
  28.2 27.0 %collective-permute-start.2 = (bf16[512,512]{1,0:T(8,128)(2,1)S(1)}, bf16[512,512]{1,0:T(8,128)(2,1)S(1)}, u32[]{:S(2)}, u32[]{:S(2)}) collective-permute-start(bf16[512,512]{1,0:T(8,128)(2,1)S(1)} %collective-permute-done), channel_id=1, source_target_pairs={{0,8},{1,33},{2,10},{3,35},{4,12},{5,37},{6,14},{7,39},{8,16},{9,4... | collective-permute-start | bytes 1572872 | tf_op jit(solution)/shard_map/ppermute | solution.py:235
  29.4 25.8 %collective-permute-start.1 = (bf16[512,512]{1,0:T(8,128)(2,1)S(1)}, bf16[512,512]{1,0:T(8,128)(2,1)S(1)}, u32[]{:S(2)}, u32[]{:S(2)}) collective-permute-start(bf16[512,512]{1,0:T(8,128)(2,1)S(1)} %collective-permute-done), channel_id=1, source_target_pairs={{0,24},{1,97},{2,26},{3,99},{4,28},{5,101},{6,30},{7,103},{8,0},{9... | collective-permute-start | bytes 1572872 | tf_op jit(solution)/shard_map/ppermute | solution.py:235
  43.3 15.1 %collective-permute-start.11 = (bf16[512,512]{1,0:T(8,128)(2,1)S(1)}, bf16[512,512]{1,0:T(8,128)(2,1)S(1)}, u32[]{:S(2)}, u32[]{:S(2)}) collective-permute-start(bf16[512,512]{1,0:T(8,128)(2,1)S(1)} %collective-permute-done.8), channel_id=1, source_target_pairs={{0,16},{1,65},{2,18},{3,67},{4,20},{5,69},{6,22},{7,71},{8,24},{9,... | collective-permute-start | bytes 1572872 | tf_op jit(solution)/shard_map/ppermute | solution.py:235
  43.3 17.7 %collective-permute-start.10 = (bf16[512,512]{1,0:T(8,128)(2,1)S(1)}, bf16[512,512]{1,0:T(8,128)(2,1)S(1)}, u32[]{:S(2)}, u32[]{:S(2)}) collective-permute-start(bf16[512,512]{1,0:T(8,128)(2,1)S(1)} %collective-permute-done.8), channel_id=1, source_target_pairs={{0,8},{1,33},{2,10},{3,35},{4,12},{5,37},{6,14},{7,39},{8,16},{9,4... | collective-permute-start | bytes 1572872 | tf_op jit(solution)/shard_map/ppermute | solution.py:235
  43.4 17.6 %collective-permute-start.9 = (bf16[512,512]{1,0:T(8,128)(2,1)S(1)}, bf16[512,512]{1,0:T(8,128)(2,1)S(1)}, u32[]{:S(2)}, u32[]{:S(2)}) collective-permute-start(bf16[512,512]{1,0:T(8,128)(2,1)S(1)} %collective-permute-done.8), channel_id=1, source_target_pairs={{0,24},{1,97},{2,26},{3,99},{4,28},{5,101},{6,30},{7,103},{8,0},{9... | collective-permute-start | bytes 1572872 | tf_op jit(solution)/shard_map/ppermute | solution.py:235
  55.5 7.1 %copy-start = (bf16[4,512,512]{2,1,0:T(8,128)(2,1)}, bf16[4,512,512]{2,1,0:T(8,128)(2,1)S(1)}, u32[]{:S(2)}) copy-start(bf16[4,512,512]{2,1,0:T(8,128)(2,1)S(1)} %pad_maximum_fusion.refs_0_) | copy-start | bytes 6291460
  55.6 37.8 %collective-permute-start.5 = (bf16[4,512,512]{2,1,0:T(8,128)(2,1)S(1)}, bf16[4,512,512]{2,1,0:T(8,128)(2,1)}, u32[]{:S(2)}, u32[]{:S(2)}) collective-permute-start(bf16[4,512,512]{2,1,0:T(8,128)(2,1)S(1)} %pad_maximum_fusion.refs_0_), channel_id=1, source_target_pairs={{0,32},{1,9},{2,34},{3,11},{4,36},{5,13},{6,38},{7,15},{8,40},{9,1... | collective-permute-start | bytes 6291464 | tf_op jit(solution)/shard_map/ppermute | solution.py:235
  55.6 37.7 %collective-permute-start.4 = (bf16[4,512,512]{2,1,0:T(8,128)(2,1)S(1)}, bf16[4,512,512]{2,1,0:T(8,128)(2,1)}, u32[]{:S(2)}, u32[]{:S(2)}) collective-permute-start(bf16[4,512,512]{2,1,0:T(8,128)(2,1)S(1)} %pad_maximum_fusion.refs_0_), channel_id=1, source_target_pairs={{0,96},{1,25},{2,98},{3,27},{4,100},{5,29},{6,102},{7,31},{8,104},... | collective-permute-start | bytes 6291464 | tf_op jit(solution)/shard_map/ppermute | solution.py:235
  62.6 53.1 %collective-permute-start.13 = (bf16[4,512,512]{2,1,0:T(8,128)(2,1)}, bf16[4,512,512]{2,1,0:T(8,128)(2,1)}, u32[]{:S(2)}, u32[]{:S(2)}) collective-permute-start(bf16[4,512,512]{2,1,0:T(8,128)(2,1)} %pad_maximum_fusion.1.refs_0_), channel_id=1, source_target_pairs={{0,32},{1,9},{2,34},{3,11},{4,36},{5,13},{6,38},{7,15},{8,40},{9,1... | collective-permute-start | bytes 6291464 | tf_op jit(solution)/shard_map/ppermute | solution.py:235
  62.7 53.1 %collective-permute-start.12 = (bf16[4,512,512]{2,1,0:T(8,128)(2,1)}, bf16[4,512,512]{2,1,0:T(8,128)(2,1)}, u32[]{:S(2)}, u32[]{:S(2)}) collective-permute-start(bf16[4,512,512]{2,1,0:T(8,128)(2,1)} %pad_maximum_fusion.1.refs_0_), channel_id=1, source_target_pairs={{0,96},{1,25},{2,98},{3,27},{4,100},{5,29},{6,102},{7,31},{8,104},... | collective-permute-start | bytes 6291464 | tf_op jit(solution)/shard_map/ppermute | solution.py:235
  95.8 41.0 %collective-permute-start.6 = (bf16[2,512,512]{2,1,0:T(8,128)(2,1)}, bf16[2,512,512]{2,1,0:T(8,128)(2,1)S(1)}, u32[]{:S(2)}, u32[]{:S(2)}) collective-permute-start(bf16[2,512,512]{2,1,0:T(8,128)(2,1)} %get-tuple-element.17), channel_id=1, source_target_pairs={{0,96},{1,25},{2,98},{3,27},{4,100},{5,29},{6,102},{7,31},{8,104},... | collective-permute-start | bytes 3145736 | tf_op jit(solution)/shard_map/ppermute | solution.py:235
  98.5 38.4 %collective-permute-start.7 = (bf16[2,512,512]{2,1,0:T(8,128)(2,1)}, bf16[2,512,512]{2,1,0:T(8,128)(2,1)S(1)}, u32[]{:S(2)}, u32[]{:S(2)}) collective-permute-start(bf16[2,512,512]{2,1,0:T(8,128)(2,1)} %get-tuple-element.18), channel_id=1, source_target_pairs={{0,32},{1,9},{2,34},{3,11},{4,36},{5,13},{6,38},{7,15},{8,40},{9,1... | collective-permute-start | bytes 3145736 | tf_op jit(solution)/shard_map/ppermute | solution.py:235
  118.2 19.3 %collective-permute-start.14 = (bf16[2,512,512]{2,1,0:T(8,128)(2,1)}, bf16[2,512,512]{2,1,0:T(8,128)(2,1)S(1)}, u32[]{:S(2)}, u32[]{:S(2)}) collective-permute-start(bf16[2,512,512]{2,1,0:T(8,128)(2,1)} %get-tuple-element.21), channel_id=1, source_target_pairs={{0,96},{1,25},{2,98},{3,27},{4,100},{5,29},{6,102},{7,31},{8,104},... | collective-permute-start | bytes 3145736 | tf_op jit(solution)/shard_map/ppermute | solution.py:235
  120.8 17.2 %collective-permute-start.15 = (bf16[2,512,512]{2,1,0:T(8,128)(2,1)}, bf16[2,512,512]{2,1,0:T(8,128)(2,1)}, u32[]{:S(2)}, u32[]{:S(2)}) collective-permute-start(bf16[2,512,512]{2,1,0:T(8,128)(2,1)} %get-tuple-element.22), channel_id=1, source_target_pairs={{0,32},{1,9},{2,34},{3,11},{4,36},{5,13},{6,38},{7,15},{8,40},{9,1... | collective-permute-start | bytes 3145736 | tf_op jit(solution)/shard_map/ppermute | solution.py:235
Sparse Core Ops, SparseCore 0:
  22.1 65.3 all-gather.2
